TPU v7x, 768 devices: a whole 4x8x12 slice. The times are simulated.
768 devices in a mesh: section: 3 (over z_hi), dp: 256 (over y, z_lo, x, core).
Axes of the slice: x: 4, y: 8, z: 12 (z_hi: 3, z_lo: 4; z = z_hi * 4 + z_lo), core: 2. Of those that a mesh axis runs over, the one named last changes fastest.
Arguments:
- hidden: bfloat16 [768, 256, 3584], P(('section', 'dp')), may hold values from -1000 to 1000, as said below
- lengths: int32 [768], P(('section', 'dp')), may hold values from 64 to 256, as said below
- pair_perm: int32 [384], replicated, may hold values from 0 to 383, as said below
- norm_gain: bfloat16 [3584], replicated, may hold values from 0.099609375 to 1.8984375
- projection: bfloat16 [3584, 1024], replicated, may hold values from -0.09375 to 0.09375
Outputs:
- hidden_grad: bfloat16 [768, 256, 3584], P(('section', 'dp'))
- loss: float32 [], replicated
Inputs may be any that keep to these rules, and one draw needn't show every extreme that they name: hidden rows of the encoder, finite. `lengths`: every sequence holds at least 64 valid tokens, and some sequence fills all 256 positions. `pair_perm`: a permutation: each docstring is paired with exactly one code.
All inputs are finite; a program needn't handle non-finite values.
Results may differ from a plain program's by a relative error of at most 0.008.
Values may be sent and summed in bfloat16 or wider, within the bound.
A program may use at most 32 MiB of HBM per device.

v0:
```python
import jax
import jax.numpy as jnp
from jax import lax
from jax.sharding import PartitionSpec as P

inv_temp = 20.0
loss_scale = 1024.0
norm_eps = 1e-06


def partners(pair_perm):
    pair_count = pair_perm.shape[0]
    order_ids = jnp.arange(pair_count, dtype=jnp.int32)
    inverse = jnp.zeros((pair_count,), jnp.int32).at[pair_perm].set(order_ids)
    return jnp.concatenate([pair_perm + pair_count, inverse])


def contract_last(left_mat, right_mat):
    return lax.dot_general(
        left_mat, right_mat, (((1,), (1,)), ((), ())), preferred_element_type=jnp.float32
    )


def body(hidden, lengths, pair_perm, norm_gain, projection):
    seq_dev = hidden.shape[0]
    width = hidden.shape[2]
    seq_count = seq_dev * lax.axis_size(("section", "dp"))
    pair_count = seq_count // 2
    device = lax.axis_index(("section", "dp"))
    first_seq = device * seq_dev
    other_start = jnp.where(first_seq >= pair_count, 0, pair_count).astype(jnp.int32)
    gain_f = norm_gain.astype(jnp.float32)
    values = hidden.astype(jnp.float32)
    inv_rms = lax.rsqrt(jnp.mean(values * values, axis=2) + norm_eps)
    positions = jnp.arange(hidden.shape[1], dtype=jnp.int32)
    share = (positions[None, :] < lengths[:, None]).astype(jnp.float32) / lengths.astype(
        jnp.float32
    )[:, None]
    pooled = (jnp.sum((share * inv_rms)[:, :, None] * values, axis=1) * gain_f[None, :]).astype(
        jnp.bfloat16
    )
    raw_emb = jnp.dot(pooled, projection, preferred_element_type=jnp.float32)
    magnitude = jnp.sqrt(jnp.sum(raw_emb * raw_emb, axis=1, keepdims=True) + norm_eps)
    unit = raw_emb / magnitude
    own_emb = unit.astype(jnp.bfloat16)
    gathered = lax.all_gather(own_emb, ("section", "dp"), axis=0, tiled=True)
    others = lax.dynamic_slice_in_dim(gathered, other_start, pair_count, 0)
    scores = inv_temp * contract_last(own_emb, others)
    exp_scores = jnp.exp(scores)
    partner_own = lax.dynamic_slice_in_dim(partners(pair_perm), first_seq, seq_dev, 0) - other_start
    columns = jnp.arange(pair_count, dtype=jnp.int32)
    target = (columns[None, :] == partner_own[:, None]).astype(jnp.float32)
    target_scores = jnp.sum(target * scores, axis=1)
    totals = jnp.sum(exp_scores, axis=1)
    own_loss = jnp.sum(jnp.log(totals)) - jnp.sum(target_scores)
    loss = lax.psum(own_loss, ("section", "dp")) / seq_count
    all_totals = lax.all_gather(totals, ("section", "dp"), axis=0, tiled=True)
    other_totals = lax.dynamic_slice_in_dim(all_totals, other_start, pair_count, 0)
    factor = loss_scale * inv_temp
    factors = exp_scores / totals[:, None] + exp_scores / other_totals[None, :] - 2.0 * target
    demb = factor * jnp.dot(factors, others.astype(jnp.float32), precision=lax.Precision.HIGHEST)
    projected = jnp.sum(unit * demb, axis=1, keepdims=True)
    grad_raw = ((demb - unit * projected) / magnitude).astype(jnp.bfloat16)
    grad_pooled = contract_last(grad_raw, projection)
    scaled = grad_pooled * gain_f[None, :]
    dot_rows = jnp.sum(values * scaled[:, None, :], axis=2)
    result = share[:, :, None] * (
        inv_rms[:, :, None] * scaled[:, None, :]
        - values * (inv_rms**3 * dot_rows / width)[:, :, None]
    )
    return (result.astype(jnp.bfloat16), loss)


def solution(mesh):
    in_specs = (P(("section", "dp"), None, None), P(("section", "dp")), P(), P(), P())
    out_specs = (P(("section", "dp"), None, None), P())
    return jax.shard_map(body, mesh=mesh, in_specs=in_specs, out_specs=out_specs, check_vma=False)
```

profile of v0, /device:TPU:1, one launch (start us, length us, event | category | flops | bytes accessed | tf_op | source)
XLA Modules:
  0.0 1272.5 jit_solution(3864476654929404140)
XLA Ops:
  7.2 0.0 copy-start.1
  7.2 0.0 all-gather.3.cloned.1.call-start
  7.9 1.9 fusion
  9.9 2.0 fusion.1
  11.9 0.0 copy-done.1
  11.9 0.0 copy-start.2
  11.9 4.1 fusion.19
  16.1 0.6 multiply_reduce_fusion.1
  17.4 0.6 fusion.18
  18.0 0.0 all-gather.3.cloned.1.call-update
  18.0 0.7 reshape.189
  18.7 0.0 copy-done.2
  18.7 2.9 scatter_custom_fusion
  21.6 0.6 dynamic_slice.11
  22.9 1119.1 %all-gather.3.cloned.1.call-done = bf16[786432]{0:T(1024)(128)(2,1)} async-done(((bf16[1024]{0:T(1024)(128)(2,1)}), bf16[786432]{0:T(1024)(128)(2,1)}) %all-gather.3.cloned.1.call-update) | async-done | bytes 1572880 | tf_op jit(solution)/shard_map/all_gather | solution.py:46
  1142.0 2.5 reshape.183
  1144.6 0.3 convolution_reduce_fusion.1
  1144.9 0.6 select_reduce_fusion
  1146.9 0.8 dynamic-update-slice
  1147.7 105.8 %all-reduce.1 = (f32[768]{0:T(1024)S(1)}, f32[]{:T(128)}) all-reduce(f32[768]{0:T(1024)S(1)} %dynamic-update-slice, f32[]{:T(128)S(6)} %sub.25), channel_id=1, replica_groups=mesh['section'=3,'dp'=256] {'section','dp'}, use_global_device_ids=true, to_apply=%add | all-reduce | flops 769 | bytes 6152
  1253.5 0.7 fusion.10
  1254.2 0.4 fusion.6
  1254.6 0.6 multiply_reduce_fusion
  1255.2 0.7 divide_convert_fusion
  1255.9 0.0 copy-start
  1255.9 5.2 convolution_reduce_fusion
  1261.2 0.0 copy-done
  1261.2 0.4 fusion.2
  1262.3 2.2 fusion.5
  (12 shorter events, 0.1 us)
Async XLA Ops:
  7.2 4.7 copy-start.1
  7.2 1134.9 %all-gather.3.cloned.1.call-start = ((), (), s32[]{:S(2)}) async-start(), calls=%async_computation | async-start | bytes 1574912 | tf_op jit(solution)/shard_map/all_gather | solution.py:46
  11.9 6.8 copy-start.2
  1255.9 5.3 copy-start
Sparse Core Ops, SparseCore 0:
  18.1 1123.8 all-gather.2
where the time goes:
time: 1270 us
  waiting for transfers between devices  1120 us (88%)
  blocking collectives  106 us (8%)
  between operations  19.3 us (2%)
    all_gather x1, waiting for transfers between devices, body(): gathered = lax.all_gather(own_emb, ('section', 'dp'), axis=0, tiled=True)  1120 us
    unnamed x1, blocking collectives  106 us
  transfers between devices with their start and end apart: 1, of which 1 were waited for; matrix products, arithmetic and copies ran while one was open for 0% of the time, Pallas kernels for 0%

commit v1 on v0

v1 whole, which is shorter than its diff:
```python
import functools

import jax
import jax.numpy as jnp
from jax import lax
from jax.experimental import pallas as pl
from jax.experimental.pallas import tpu as pltpu
from jax.sharding import PartitionSpec as P

MESH = pl.DeviceIdType.MESH
ANY = pl.BlockSpec(memory_space=pl.ANY)
SMEM = pl.BlockSpec(memory_space=pltpu.SMEM)
VMEM = pl.BlockSpec(memory_space=pltpu.VMEM)
bf16, f32 = jnp.bfloat16, jnp.float32

INV_TEMP = 20.0
LOSS_SCALE = 1024.0
EPS = 1e-06

NX, NY, NZ = 4, 8, 12
ROWS = 64
PROJ = 512

XC = [(x, 0, 0, c) for x in range(NX) for c in range(2) if (x, c) != (0, 0)]
FAR = [(0, y, z, 0) for z in (0, 4, 8) for y in (0, 2, 4, 6) if (y, z) != (0, 0)]
ZNEAR = [(0, 0, 1, 0), (0, 0, -1, 0), (0, 0, 2, 0), (0, 0, -2, 0)]
YNEAR = [(0, 1, 0, 0), (0, -1, 0, 0)]
PEERS = XC + FAR + ZNEAR + YNEAR
N_COPIES = len(XC) + len(FAR) + len(ZNEAR) + 4 * len(YNEAR) + 8


def contract_last(a, b):
    return lax.dot_general(a, b, (((1,), (1,)), ((), ())), preferred_element_type=f32)


def split3(v):
    hi = v.astype(bf16)
    rest = v - hi.astype(f32)
    mid = rest.astype(bf16)
    return hi, mid, (rest - mid.astype(f32)).astype(bf16)


def stack3(row):
    hi, mid, lo = split3(jnp.broadcast_to(row, (16, row.shape[1])))
    i = lax.broadcasted_iota(jnp.int32, hi.shape, 0)
    zero = jnp.zeros_like(hi)
    return jnp.where(i == 0, hi, jnp.where(i == 1, mid, jnp.where(i == 2, lo, zero)))


def main_kernel(
    hidden, lengths, perm_s, perm_v, gain_h, proj_h,
    g_out, coef_out, loss_out,
    x_v, proj, proj_t, gain_v, packets, emb, target, pooled_v,
    in_sem, send_sem, recv_sem,
):
    z_hi = lax.axis_index("section")
    dp = lax.axis_index("dp")
    core = dp % 2
    x = (dp // 2) % NX
    z_lo = (dp // (2 * NX)) % 4
    y = dp // (8 * NX)
    z = z_hi * 4 + z_lo
    y_far, y_par = y // 2, y % 2

    def device(d):
        xx = (x + d[0]) % NX
        yy = (y + d[1] + NY) % NY
        zz = (z + d[2] + NZ) % NZ
        cc = (core + d[3]) % 2
        return (zz // 4, ((yy * 4 + zz % 4) * NX + xx) * 2 + cc)

    barrier = pltpu.get_barrier_semaphore()

    width = x_v.shape[1]
    length_rows = x_v.shape[0]
    n_x, n_p = length_rows // ROWS, width // PROJ
    loads = [
        pltpu.make_async_copy(
            hidden.at[0, pl.ds(i * ROWS, ROWS)], x_v.at[pl.ds(i * ROWS, ROWS)], in_sem.at[i]
        )
        for i in range(n_x)
    ]
    loads.append(pltpu.make_async_copy(gain_h, gain_v, in_sem.at[n_x]))
    loads += [
        pltpu.make_async_copy(
            proj_h.at[pl.ds(i * PROJ, PROJ)], proj.at[pl.ds(i * PROJ, PROJ)], in_sem.at[n_x + 1 + i]
        )
        for i in range(n_p)
    ]
    for load in loads:
        load.start()
    for d in PEERS:
        pl.semaphore_signal(barrier, inc=1, device_id=device(d), device_id_type=MESH)

    length = lengths[0]
    inv_len = 1.0 / jnp.full((1, 1), length, jnp.int32).astype(f32)
    pooled = jnp.zeros((1, width), f32)
    for i in range(n_x):
        loads[i].wait()
        rows = pl.ds(i * ROWS, ROWS)
        sums = jnp.zeros((ROWS, 128), f32)
        for k in range(width // 128):
            v = x_v[rows, k * 128 : (k + 1) * 128].astype(f32)
            sums = sums + v * v
        inv_rms = lax.rsqrt(jnp.sum(sums, axis=1, keepdims=True) / width + EPS)
        position = lax.broadcasted_iota(jnp.int32, (ROWS, 1), 0) + i * ROWS
        share = jnp.where(position < length, inv_len, 0.0)
        weight = share * inv_rms
        cubed = weight * inv_rms * inv_rms / width
        lane = lax.broadcasted_iota(jnp.int32, (ROWS, 128), 1)
        coef_out[rows, :] = jnp.where(lane == 0, weight, cubed)
        weight_row = jnp.broadcast_to(weight, (ROWS, 128)).T[0:1, :]
        parts = jnp.dot(stack3(weight_row), x_v[rows, :], preferred_element_type=f32)
        pooled = pooled + (parts[0:1] + (parts[1:2] + parts[2:3]))
    loads[n_x].wait()
    gain = gain_v[...].astype(f32).reshape(1, width)
    pooled_v[...] = jnp.broadcast_to(pooled * gain, (16, width)).astype(bf16)

    raw = jnp.zeros((16, proj.shape[1]), f32)
    for i in range(n_p):
        loads[n_x + 1 + i].wait()
        cut = slice(i * PROJ, (i + 1) * PROJ)
        raw = raw + jnp.dot(pooled_v[:, cut], proj[cut, :], preferred_element_type=f32)
    raw = raw[0:8]
    magnitude = jnp.sqrt(jnp.sum(raw * raw, axis=1, keepdims=True) + EPS)
    unit = raw / magnitude
    own = unit.astype(bf16)
    sub = lax.broadcasted_iota(jnp.int32, (8, 128), 0)
    packet = jnp.zeros((8, 128), f32)
    for k in range(8):
        packet = jnp.where(sub == k, own[:, k * 128 : (k + 1) * 128].astype(f32), packet)
    mine = x * 2 + core
    my_rows = pl.ds(pl.multiple_of(mine * 8, 8), 8)
    packets[my_rows, :] = packet

    count = [0]

    def copy(src, dst, d):
        k = count[0]
        count[0] += 1
        out = pltpu.make_async_remote_copy(
            src_ref=src, dst_ref=dst, send_sem=send_sem.at[k], recv_sem=recv_sem.at[k],
            device_id=device(d), device_id_type=MESH,
        )
        out.start()
        sent.append(out)
        return out

    sent = []
    half = pl.multiple_of(core * 512, 512)
    all_half = pl.ds(half, 512)
    quarters = [pl.ds(half, 256), pl.ds(pl.multiple_of(half + 256, 256), 256)]

    pl.semaphore_wait(barrier, len(PEERS))
    phase1 = [copy(packets.at[my_rows], packets.at[my_rows], d) for d in XC]
    for c in phase1:
        c.wait_recv()
    block = emb.at[z_hi, y_far, y_par, z_lo]
    for k in range(8):
        @pl.when(k // 4 == core)
        def _(k=k):
            part = packets[pl.ds(k, 8, stride=8), :]
            block[:, k * 128 : (k + 1) * 128] = part.astype(bf16)
    cut = emb.at[z_hi, y_far, y_par, z_lo, :, all_half]
    phase2 = [copy(cut, cut, d) for d in FAR]

    def transpose(i, _):
        at = pl.ds(pl.multiple_of(i * 256, 256), 256)
        proj_t[:, at] = proj[at, :].T
        return 0

    lax.fori_loop(0, width // 256, transpose, 0)
    pairs = target.shape[0]
    perm_row = perm_v[...].astype(f32).reshape(1, pairs)
    perm_col = jnp.broadcast_to(perm_row, (128, pairs)).T[:, 0:1]
    column = lax.broadcasted_iota(jnp.int32, (pairs, pairs), 1).astype(f32)
    target[...] = jnp.where(column == perm_col, 1.0, 0.0)

    for c in phase2:
        c.wait_recv()

    def znear(k):
        cols = all_half if k < 2 else quarters[k - 2]
        part = emb.at[:, :, y_par, z_lo, :, cols]
        return copy(part, part, ZNEAR[k])

    def ynear(zl):
        out = []
        for k in range(2):
            part = emb.at[:, :, y_par, zl, :, quarters[k]]
            out.append(copy(part, part, YNEAR[k]))
        return out

    def sibling(par, zl):
        part = emb.at[:, :, par, zl, :, all_half]
        return copy(part, part, (0, 0, 0, 1))

    phase3 = [znear(k) for k in range(4)]
    classes = [z_lo, (z_lo + 3) % 4, (z_lo + 1) % 4, (z_lo + 2) % 4]
    phase4, phase5 = [ynear(classes[0])], [sibling(y_par, classes[0])]
    for k in (1, 2, 3):
        for c in phase3[k - 1 : k] if k < 3 else phase3[2:]:
            c.wait_recv()
        phase4.append(ynear(classes[k]))
        phase5.append(sibling(y_par, classes[k]))
    for k in range(4):
        for c in phase4[k]:
            c.wait_recv()
        phase5.append(sibling(1 - y_par, classes[k]))
    for c in phase5:
        c.wait_recv()
    for c in sent:
        c.wait_send()

    everyone = emb[...].reshape(2 * pairs, emb.shape[-1])
    codes, docs = everyone[:pairs], everyone[pairs:]
    scores = INV_TEMP * contract_last(codes, docs)
    exps = jnp.exp(scores)
    code_totals = jnp.sum(exps, axis=1, keepdims=True)
    doc_totals = jnp.sum(exps, axis=0, keepdims=True)
    log_sum = jnp.sum(jnp.log(doc_totals)) + jnp.sum(jnp.log(code_totals))
    loss_out[0, 0] = (log_sum - 2.0 * jnp.sum(target[...] * scores)) / (2 * pairs)
    code_row = jnp.broadcast_to(code_totals, (pairs, 128)).T[0:1, :]

    me = z_hi * (pairs * 2 // 3) + dp
    is_code = me < pairs
    other_totals = jnp.where(is_code, doc_totals, code_row)
    other_blocks = jnp.where(is_code, pairs // 8, 0)
    flat = emb.reshape(2 * pairs // 8, 8, emb.shape[-1])
    others = flat[pl.ds(other_blocks, pairs // 8)].reshape(pairs, emb.shape[-1])
    own_exps = jnp.exp(INV_TEMP * contract_last(own, others)[0:1, :])
    own_total = jnp.sum(own_exps, axis=1, keepdims=True)
    columns = lax.broadcasted_iota(jnp.int32, (1, pairs), 1)
    code_id = jnp.where(is_code, me, 0)
    doc_id = jnp.where(is_code, 0, me - pairs)
    code_hit = columns == jnp.full((1, 1), perm_s[code_id], jnp.int32)
    doc_hit = perm_row == jnp.full((1, 1), doc_id, jnp.int32).astype(f32)
    hit = jnp.where(is_code, jnp.where(code_hit, 1.0, 0.0), jnp.where(doc_hit, 1.0, 0.0))
    factors = own_exps / own_total + own_exps / other_totals - 2.0 * hit
    terms = jnp.dot(stack3(factors), others, preferred_element_type=f32)
    demb = (LOSS_SCALE * INV_TEMP) * (terms[0:1] + (terms[1:2] + terms[2:3]))
    unit_row = unit[0:1]
    projected = jnp.sum(unit_row * demb, axis=1, keepdims=True)
    grad_raw = (demb - unit_row * projected) / magnitude[0:1]
    grad_rows = jnp.broadcast_to(grad_raw, (16, grad_raw.shape[1])).astype(bf16)
    grad_pooled = jnp.dot(grad_rows, proj_t[...], preferred_element_type=f32)
    g_out[...] = grad_pooled[0:1] * gain


def out_kernel(hidden, g, coef, out):
    rows = hidden[0]
    terms = contract_last(rows, stack3(g[...]))
    dots = terms[:, 0:1] + (terms[:, 1:2] + terms[:, 2:3])
    weight = coef[:, 0:1]
    cubed = coef[:, 1:2] * dots
    out[0] = (weight * g[...] - rows.astype(f32) * cubed).astype(bf16)


def body(hidden, lengths, pair_perm, norm_gain, projection):
    _, length_rows, width = hidden.shape
    embed = projection.shape[1]
    pairs = pair_perm.shape[0]
    g, coef, loss = pl.pallas_call(
        main_kernel,
        out_shape=(
            jax.ShapeDtypeStruct((1, width), f32),
            jax.ShapeDtypeStruct((length_rows, 128), f32),
            jax.ShapeDtypeStruct((1, 1), f32),
        ),
        in_specs=[ANY, SMEM, SMEM, VMEM, ANY, ANY],
        out_specs=(VMEM, VMEM, SMEM),
        scratch_shapes=[
            pltpu.VMEM((length_rows, width), bf16),
            pltpu.VMEM((width, embed), bf16),
            pltpu.VMEM((embed, width), bf16),
            pltpu.VMEM((width,), bf16),
            pltpu.VMEM((64, 128), f32),
            pltpu.VMEM((3, 4, 2, 4, 8, embed), bf16),
            pltpu.VMEM((pairs, pairs), f32),
            pltpu.VMEM((16, width), bf16),
            pltpu.SemaphoreType.DMA((length_rows // ROWS + 1 + width // PROJ,)),
            pltpu.SemaphoreType.DMA((N_COPIES,)),
            pltpu.SemaphoreType.DMA((N_COPIES,)),
        ],
        compiler_params=pltpu.CompilerParams(
            collective_id=0, has_side_effects=True, vmem_limit_bytes=48 << 20
        ),
        name="main",
    )(hidden, lengths, pair_perm, pair_perm, norm_gain, projection)
    grad = pl.pallas_call(
        out_kernel,
        grid=(length_rows // ROWS,),
        out_shape=jax.ShapeDtypeStruct(hidden.shape, bf16),
        in_specs=[
            pl.BlockSpec((1, ROWS, width), lambda i: (0, i, 0)),
            pl.BlockSpec((1, width), lambda i: (0, 0)),
            pl.BlockSpec((ROWS, 128), lambda i: (i, 0)),
        ],
        out_specs=pl.BlockSpec((1, ROWS, width), lambda i: (0, i, 0)),
        compiler_params=pltpu.CompilerParams(vmem_limit_bytes=32 << 20),
        name="hidden_grad",
    )(hidden, g, coef)
    return grad, loss.reshape(())


def solution(mesh):
    in_specs = (P(("section", "dp"), None, None), P(("section", "dp")), P(), P(), P())
    out_specs = (P(("section", "dp"), None, None), P())
    return jax.shard_map(body, mesh=mesh, in_specs=in_specs, out_specs=out_specs, check_vma=False)
```

time: 1270 us -> 60.8 us (0.05)
  waiting for transfers between devices: 1120 us -> 0 us
  blocking collectives: 106 us -> 0 us
  Pallas kernels: 0 us -> 54.6 us
  between operations: 19.3 us -> 3.03 us
    all_gather x1 -> x0, waiting for transfers between devices: 1120 us -> none  [body(): gathered = lax.all_gather(own_emb, ('section', 'dp'), axis=0, tiled=True)]
    unnamed x1 -> x0, blocking collectives: 106 us -> none
    pallas_call x0 -> x2, Pallas kernels: none -> 54.6 us  [the longest x1 51.1 us: body(): pl.pallas_call(main_kernel, out_shape=(jax.ShapeDtypeStruct((1, width), f...]
  transfers between devices with their start and end apart: 1 -> 0, of which waited for: 1 -> 0; matrix products, arithmetic and copies ran while one was open for 0% -> 0% of each run, Pallas kernels for 0% -> 0%
where the time goes in v1:
time: 60.8 us; the launch traced here: 60.5 us
  Pallas kernels  54.6 us (90%)
  between operations  3.03 us (5%)
  local copies, waits for them, and re-layouts  2.87 us (5%)
    pallas_call x1, Pallas kernels, body(): pl.pallas_call(main_kernel, out_shape=(jax.ShapeDtypeStruct((1, width), f...  51.1 us
    pallas_call x1, Pallas kernels, body(): pl.pallas_call(out_kernel, grid=(length_rows // ROWS,), out_shape=jax.Sha...  3.48 us
    unnamed x6, local copies, waits for them, and re-layouts  2.87 us

profile of v1, /device:TPU:1, one launch (start us, length us, event | category | flops | bytes accessed | tf_op | source)
XLA Modules:
  0.0 60.5 jit_solution(11157256761878186054)
XLA Ops:
  1.3 0.0 copy-start
  1.3 1.5 %copy-done = bf16[1,256,3584]{2,1,0:T(8,128)(2,1)S(1)} copy-done((bf16[1,256,3584]{2,1,0:T(8,128)(2,1)S(1)}, bf16[1,256,3584]{2,1,0:T(8,128)(2,1)}, u32[]{:S(2)}) %copy-start) | copy-done | bytes 1835032
  2.8 0.0 copy-start.1
  2.8 0.7 %copy-done.1 = bf16[3584]{0:T(1024)(128)(2,1)S(1)} copy-done((bf16[3584]{0:T(1024)(128)(2,1)S(1)}, bf16[3584]{0:T(1024)(128)(2,1)}, u32[]{:S(2)}) %copy-start.1) | copy-done | bytes 7192
  3.5 0.0 copy-start.2
  3.5 0.7 %copy-done.2 = s32[384]{0:T(512)S(1)} copy-done((s32[384]{0:T(512)S(1)}, s32[384]{0:T(512)}, u32[]{:S(2)}) %copy-start.2) | copy-done | bytes 1560
  4.2 51.1 %main.1 = (f32[1,3584]{1,0:T(1,128)S(1)}, f32[256,128]{1,0:T(8,128)S(1)}, f32[1,1]{1,0:T(1,128)}) custom-call(bf16[1,256,3584]{2,1,0:T(8,128)(2,1)S(1)} %copy-done, s32[1]{0:T(128)S(6)} %copy.8.lengths, s32[384]{0:T(512)S(1)} %copy-done.2, s32[384]{0:T(512)S(1)} %copy-done.2, bf16[3584]{0:T(1024)(128)(2,1)S(1)} %copy-done.1, bf16[3584,1024]{1,0:T(8,128)(2,1)} %proj_h.1), custom_call_target="tpu_custom_call" | custom-call | tf_op jit(solution)/shard_map/main/pallas_call | solution.py:263
  55.3 3.5 %hidden_grad.1 = bf16[1,256,3584]{2,1,0:T(8,128)(2,1)} custom-call(bf16[1,256,3584]{2,1,0:T(8,128)(2,1)S(1)} %copy-done, f32[1,3584]{1,0:T(1,128)S(1)} %get-tuple-element.5.g, f32[256,128]{1,0:T(8,128)S(1)} %get-tuple-element.6.coef), custom_call_target="tpu_custom_call" | custom-call | tf_op jit(solution)/shard_map/hidden_grad/pallas_call | solution.py:290
Async XLA Ops:
  1.3 1.5 %copy-start = (bf16[1,256,3584]{2,1,0:T(8,128)(2,1)S(1)}, bf16[1,256,3584]{2,1,0:T(8,128)(2,1)}, u32[]{:S(2)}) copy-start(bf16[1,256,3584]{2,1,0:T(8,128)(2,1)} %hidden.3) | copy-start | bytes 5505028
  2.8 0.7 %copy-start.1 = (bf16[3584]{0:T(1024)(128)(2,1)S(1)}, bf16[3584]{0:T(1024)(128)(2,1)}, u32[]{:S(2)}) copy-start(bf16[3584]{0:T(1024)(128)(2,1)} %gain_h.1) | copy-start | bytes 21508
  3.5 0.7 %copy-start.2 = (s32[384]{0:T(512)S(1)}, s32[384]{0:T(512)}, u32[]{:S(2)}) copy-start(s32[384]{0:T(512)} %perm_v.1) | copy-start | bytes 4612

commit v2 on v1

--- a/solution.py
+++ b/solution.py
@@ -8,7 +8,7 @@
 from jax.sharding import PartitionSpec as P
 
 MESH = pl.DeviceIdType.MESH
-ANY = pl.BlockSpec(memory_space=pl.ANY)
+HBM = pl.BlockSpec(memory_space=pltpu.HBM)
 SMEM = pl.BlockSpec(memory_space=pltpu.SMEM)
 VMEM = pl.BlockSpec(memory_space=pltpu.VMEM)
 bf16, f32 = jnp.bfloat16, jnp.float32
@@ -22,11 +22,30 @@
 PROJ = 512
 
 XC = [(x, 0, 0, c) for x in range(NX) for c in range(2) if (x, c) != (0, 0)]
-FAR = [(0, y, z, 0) for z in (0, 4, 8) for y in (0, 2, 4, 6) if (y, z) != (0, 0)]
-ZNEAR = [(0, 0, 1, 0), (0, 0, -1, 0), (0, 0, 2, 0), (0, 0, -2, 0)]
-YNEAR = [(0, 1, 0, 0), (0, -1, 0, 0)]
-PEERS = XC + FAR + ZNEAR + YNEAR
-N_COPIES = len(XC) + len(FAR) + len(ZNEAR) + 4 * len(YNEAR) + 8
+FAR = [(0, 4, 4), (0, 4, 8), (0, 2, 4), (0, 2, 8), (0, 6, 4), (0, 6, 8), (0, 4, 0)]
+FAR += [(0, 0, 4), (0, 0, 8), (0, 2, 0), (0, 6, 0)]
+FIRST, SECOND, WHOLE = (0, 2), (2, 2), (0, 4)
+MID = [
+    ((0, 1), [((1, 0, 1), WHOLE)]),
+    ((0, -1), [((3, 0, -1), WHOLE)]),
+    ((1, 1), [((3, 1, 1), FIRST), ((3, -1, 1), SECOND)]),
+    ((1, -1), [((1, 1, -1), FIRST), ((1, -1, -1), SECOND)]),
+    ((1, 0), [((2, 1, 0), FIRST), ((2, -1, 0), SECOND)]),
+    ((1, 2), [((0, 1, 2), FIRST), ((0, -1, -2), SECOND)]),
+    ((0, 2), [((2, 0, 2), FIRST), ((2, 0, -2), SECOND)]),
+]
+LAST = [
+    ((1, 0, 0), FIRST), ((3, 0, 0), FIRST), ((0, 0, 1), SECOND),
+    ((0, 0, -1), SECOND), ((0, 1, 0), FIRST), ((0, -1, 0), SECOND),
+]
+SIBLING = (0, 0, 0, 1)
+OTHER_CHIPS = FAR + [d for _, copies in MID for d, _ in copies] + [d for d, _ in LAST]
+PEERS = sorted({(x, y % NY, z % NZ, c) for x, y, z, c in XC + [(*d, 0) for d in OTHER_CHIPS]})
+AT_FAR = len(XC)
+AT_MID = AT_FAR + len(FAR)
+AT_LAST = AT_MID + 2 * len(MID)
+AT_SIB = AT_LAST + 8 * len(LAST)
+N_COPIES = AT_SIB + 8
 
 
 def contract_last(a, b):
@@ -48,10 +67,10 @@
 
 
 def main_kernel(
-    hidden, lengths, perm_s, perm_v, gain_h, proj_h,
+    hidden, lengths_h, perm_h, gain_h, proj_h,
     g_out, coef_out, loss_out,
-    x_v, proj, proj_t, gain_v, packets, emb, target, pooled_v,
-    in_sem, send_sem, recv_sem,
+    lengths, perm_s, perm_v, x_v, proj, proj_t, gain_v, gain_f, packets, emb, target, pooled_v, xg_proj,
+    in_sem, small_sem, send_sem, recv_sem,
 ):
     z_hi = lax.axis_index("section")
     dp = lax.axis_index("dp")
@@ -66,7 +85,7 @@
         xx = (x + d[0]) % NX
         yy = (y + d[1] + NY) % NY
         zz = (z + d[2] + NZ) % NZ
-        cc = (core + d[3]) % 2
+        cc = (core + d[3]) % 2 if len(d) == 4 else core
         return (zz // 4, ((yy * 4 + zz % 4) * NX + xx) * 2 + cc)
 
     barrier = pltpu.get_barrier_semaphore()
@@ -80,18 +99,24 @@
         )
         for i in range(n_x)
     ]
-    loads.append(pltpu.make_async_copy(gain_h, gain_v, in_sem.at[n_x]))
     loads += [
         pltpu.make_async_copy(
-            proj_h.at[pl.ds(i * PROJ, PROJ)], proj.at[pl.ds(i * PROJ, PROJ)], in_sem.at[n_x + 1 + i]
+            proj_h.at[pl.ds(i * PROJ, PROJ)], proj.at[pl.ds(i * PROJ, PROJ)], in_sem.at[n_x + i]
         )
         for i in range(n_p)
     ]
-    for load in loads:
+    small = [
+        pltpu.make_async_copy(src, dst, small_sem.at[i])
+        for i, (src, dst) in enumerate(
+            ((lengths_h, lengths), (gain_h, gain_v), (perm_h, perm_s), (perm_h, perm_v))
+        )
+    ]
+    for load in small + loads:
         load.start()
     for d in PEERS:
         pl.semaphore_signal(barrier, inc=1, device_id=device(d), device_id_type=MESH)
 
+    small[0].wait()
     length = lengths[0]
     inv_len = 1.0 / jnp.full((1, 1), length, jnp.int32).astype(f32)
     pooled = jnp.zeros((1, width), f32)
@@ -112,13 +137,14 @@
         weight_row = jnp.broadcast_to(weight, (ROWS, 128)).T[0:1, :]
         parts = jnp.dot(stack3(weight_row), x_v[rows, :], preferred_element_type=f32)
         pooled = pooled + (parts[0:1] + (parts[1:2] + parts[2:3]))
-    loads[n_x].wait()
-    gain = gain_v[...].astype(f32).reshape(1, width)
+    small[1].wait()
+    gain_f[...] = gain_v[...].astype(f32).reshape(1, width)
+    gain = gain_f[...]
     pooled_v[...] = jnp.broadcast_to(pooled * gain, (16, width)).astype(bf16)
 
     raw = jnp.zeros((16, proj.shape[1]), f32)
     for i in range(n_p):
-        loads[n_x + 1 + i].wait()
+        loads[n_x + i].wait()
         cut = slice(i * PROJ, (i + 1) * PROJ)
         raw = raw + jnp.dot(pooled_v[:, cut], proj[cut, :], preferred_element_type=f32)
     raw = raw[0:8]
@@ -133,84 +159,97 @@
     my_rows = pl.ds(pl.multiple_of(mine * 8, 8), 8)
     packets[my_rows, :] = packet
 
-    count = [0]
-
-    def copy(src, dst, d):
-        k = count[0]
-        count[0] += 1
+    for c in small[2:]:
+        c.wait()
+    pairs = target.shape[0]
+    perm_row = perm_v[...].astype(f32).reshape(1, pairs)
+
+    def prepare():
+        def transpose(i, _):
+            at = pl.ds(pl.multiple_of(i * 256, 256), 256)
+            proj_t[:, at] = proj[at, :].T
+            return 0
+
+        lax.fori_loop(0, width // 256, transpose, 0)
+        perm_col = jnp.broadcast_to(perm_row, (128, pairs)).T[:, 0:1]
+        column = lax.broadcasted_iota(jnp.int32, (pairs, pairs), 1).astype(f32)
+        target[...] = jnp.where(column == perm_col, 1.0, 0.0)
+        xg_proj[...] = jnp.zeros_like(xg_proj)
+
+        def gained(i, _):
+            at = pl.ds(pl.multiple_of(i * PROJ, PROJ), PROJ)
+            xg = x_v[:, at].astype(f32) * gain_f[:, at]
+            high = xg.astype(bf16)
+            low = (xg - high.astype(f32)).astype(bf16)
+            both = jnp.dot(
+                jnp.concatenate([high, low], axis=0), proj[at, :], preferred_element_type=f32
+            )
+            xg_proj[...] += both[:length_rows] + both[length_rows:]
+            return 0
+
+        lax.fori_loop(0, n_p, gained, 0)
+
+    pl.when(z_hi == 0)(prepare)
+
+    sent = []
+
+    def copy(k, ref, d):
         out = pltpu.make_async_remote_copy(
-            src_ref=src, dst_ref=dst, send_sem=send_sem.at[k], recv_sem=recv_sem.at[k],
+            src_ref=ref, dst_ref=ref, send_sem=send_sem.at[k], recv_sem=recv_sem.at[k],
             device_id=device(d), device_id_type=MESH,
         )
         out.start()
         sent.append(out)
         return out
 
-    sent = []
-    half = pl.multiple_of(core * 512, 512)
-    all_half = pl.ds(half, 512)
-    quarters = [pl.ds(half, 256), pl.ds(pl.multiple_of(half + 256, 256), 256)]
+    def tile(q):
+        return pl.ds(pl.multiple_of(core * 512 + (q % 4) * 128, 128), 128)
 
     pl.semaphore_wait(barrier, len(PEERS))
-    phase1 = [copy(packets.at[my_rows], packets.at[my_rows], d) for d in XC]
-    for c in phase1:
+    arriving = [copy(i, packets.at[my_rows], d) for i, d in enumerate(XC)]
+    for c in arriving:
         c.wait_recv()
     block = emb.at[z_hi, y_far, y_par, z_lo]
     for k in range(8):
-        @pl.when(k // 4 == core)
+        @pl.when(k == core * 4 + x)
         def _(k=k):
             part = packets[pl.ds(k, 8, stride=8), :]
             block[:, k * 128 : (k + 1) * 128] = part.astype(bf16)
-    cut = emb.at[z_hi, y_far, y_par, z_lo, :, all_half]
-    phase2 = [copy(cut, cut, d) for d in FAR]
-
-    def transpose(i, _):
-        at = pl.ds(pl.multiple_of(i * 256, 256), 256)
-        proj_t[:, at] = proj[at, :].T
-        return 0
-
-    lax.fori_loop(0, width // 256, transpose, 0)
-    pairs = target.shape[0]
-    perm_row = perm_v[...].astype(f32).reshape(1, pairs)
-    perm_col = jnp.broadcast_to(perm_row, (128, pairs)).T[:, 0:1]
-    column = lax.broadcasted_iota(jnp.int32, (pairs, pairs), 1).astype(f32)
-    target[...] = jnp.where(column == perm_col, 1.0, 0.0)
-
-    for c in phase2:
+
+    cut = emb.at[z_hi, y_far, y_par, z_lo, :, tile(x)]
+    arriving = [copy(AT_FAR + i, cut, d) for i, d in enumerate(FAR)]
+    for c in arriving:
         c.wait_recv()
 
-    def znear(k):
-        cols = all_half if k < 2 else quarters[k - 2]
-        part = emb.at[:, :, y_par, z_lo, :, cols]
-        return copy(part, part, ZNEAR[k])
-
-    def ynear(zl):
-        out = []
-        for k in range(2):
-            part = emb.at[:, :, y_par, zl, :, quarters[k]]
-            out.append(copy(part, part, YNEAR[k]))
-        return out
-
-    def sibling(par, zl):
-        part = emb.at[:, :, par, zl, :, all_half]
-        return copy(part, part, (0, 0, 0, 1))
-
-    phase3 = [znear(k) for k in range(4)]
-    classes = [z_lo, (z_lo + 3) % 4, (z_lo + 1) % 4, (z_lo + 2) % 4]
-    phase4, phase5 = [ynear(classes[0])], [sibling(y_par, classes[0])]
-    for k in (1, 2, 3):
-        for c in phase3[k - 1 : k] if k < 3 else phase3[2:]:
+    near = []
+    for i, (_, copies) in enumerate(MID):
+        near.append([
+            copy(AT_MID + 2 * i + j, emb.at[:, pl.ds(*part), y_par, z_lo, :, tile(x)], d)
+            for j, (d, part) in enumerate(copies)
+        ])
+
+    held = x - 2 * y - z + 32
+    classes = [(y_par, z_lo)]
+    classes += [((y_par + dy) % 2, (z_lo - dz + 4) % 4) for (dy, dz), _ in MID]
+    neighbours = []
+    for i, (par, lo) in enumerate(classes):
+        for c in near[i - 1] if i else ():
             c.wait_recv()
-        phase4.append(ynear(classes[k]))
-        phase5.append(sibling(y_par, classes[k]))
-    for k in range(4):
-        for c in phase4[k]:
+        base = AT_LAST + len(LAST) * (4 * par + lo)
+        cols = tile(held + 2 * par + lo)
+        neighbours.append([
+            copy(base + j, emb.at[:, pl.ds(*part), par, lo, :, cols], d)
+            for j, (d, part) in enumerate(LAST)
+        ])
+    half = pl.ds(pl.multiple_of(core * 512, 512), 512)
+    arriving = []
+    for i, (par, lo) in enumerate(classes):
+        for c in neighbours[i]:
             c.wait_recv()
-        phase5.append(sibling(1 - y_par, classes[k]))
-    for c in phase5:
+        arriving.append(copy(AT_SIB + 4 * par + lo, emb.at[:, :, par, lo, :, half], SIBLING))
+    pl.when(z_hi != 0)(prepare)
+    for c in arriving:
         c.wait_recv()
-    for c in sent:
-        c.wait_send()
 
     everyone = emb[...].reshape(2 * pairs, emb.shape[-1])
     codes, docs = everyone[:pairs], everyone[pairs:]
@@ -244,16 +283,16 @@
     grad_raw = (demb - unit_row * projected) / magnitude[0:1]
     grad_rows = jnp.broadcast_to(grad_raw, (16, grad_raw.shape[1])).astype(bf16)
     grad_pooled = jnp.dot(grad_rows, proj_t[...], preferred_element_type=f32)
-    g_out[...] = grad_pooled[0:1] * gain
+    g_out[...] = grad_pooled[0:1] * gain_f[...]
+    dots = jnp.sum(xg_proj[...] * grad_rows[0:1].astype(f32), axis=1, keepdims=True)
+    lane = lax.broadcasted_iota(jnp.int32, coef_out.shape, 1)
+    coef_out[...] = jnp.where(lane == 1, coef_out[...] * dots, coef_out[...])
+    for c in sent:
+        c.wait_send()
 
 
 def out_kernel(hidden, g, coef, out):
-    rows = hidden[0]
-    terms = contract_last(rows, stack3(g[...]))
-    dots = terms[:, 0:1] + (terms[:, 1:2] + terms[:, 2:3])
-    weight = coef[:, 0:1]
-    cubed = coef[:, 1:2] * dots
-    out[0] = (weight * g[...] - rows.astype(f32) * cubed).astype(bf16)
+    out[0] = (coef[:, 0:1] * g[...] - hidden[0].astype(f32) * coef[:, 1:2]).astype(bf16)
 
 
 def body(hidden, lengths, pair_perm, norm_gain, projection):
@@ -267,26 +306,32 @@
             jax.ShapeDtypeStruct((length_rows, 128), f32),
             jax.ShapeDtypeStruct((1, 1), f32),
         ),
-        in_specs=[ANY, SMEM, SMEM, VMEM, ANY, ANY],
+        in_specs=[HBM] * 5,
         out_specs=(VMEM, VMEM, SMEM),
         scratch_shapes=[
+            pltpu.SMEM(lengths.shape, jnp.int32),
+            pltpu.SMEM(pair_perm.shape, jnp.int32),
+            pltpu.VMEM(pair_perm.shape, jnp.int32),
             pltpu.VMEM((length_rows, width), bf16),
             pltpu.VMEM((width, embed), bf16),
             pltpu.VMEM((embed, width), bf16),
             pltpu.VMEM((width,), bf16),
+            pltpu.VMEM((1, width), f32),
             pltpu.VMEM((64, 128), f32),
             pltpu.VMEM((3, 4, 2, 4, 8, embed), bf16),
             pltpu.VMEM((pairs, pairs), f32),
             pltpu.VMEM((16, width), bf16),
-            pltpu.SemaphoreType.DMA((length_rows // ROWS + 1 + width // PROJ,)),
+            pltpu.VMEM((length_rows, embed), f32),
+            pltpu.SemaphoreType.DMA((length_rows // ROWS + width // PROJ,)),
+            pltpu.SemaphoreType.DMA((4,)),
             pltpu.SemaphoreType.DMA((N_COPIES,)),
             pltpu.SemaphoreType.DMA((N_COPIES,)),
         ],
         compiler_params=pltpu.CompilerParams(
-            collective_id=0, has_side_effects=True, vmem_limit_bytes=48 << 20
+            collective_id=0, has_side_effects=True, vmem_limit_bytes=60 << 20
         ),
         name="main",
-    )(hidden, lengths, pair_perm, pair_perm, norm_gain, projection)
+    )(hidden, lengths, pair_perm, norm_gain, projection)
     grad = pl.pallas_call(
         out_kernel,
         grid=(length_rows // ROWS,),
@@ -297,7 +342,7 @@
             pl.BlockSpec((ROWS, 128), lambda i: (i, 0)),
         ],
         out_specs=pl.BlockSpec((1, ROWS, width), lambda i: (0, i, 0)),
-        compiler_params=pltpu.CompilerParams(vmem_limit_bytes=32 << 20),
+        compiler_params=pltpu.CompilerParams(vmem_limit_bytes=60 << 20),
         name="hidden_grad",
     )(hidden, g, coef)
     return grad, loss.reshape(())

time: 60.8 us -> 55.3 us (0.910)
  local copies, waits for them, and re-layouts: 2.87 us -> 0 us
  Pallas kernels: 54.6 us -> 52.1 us
    pallas_call x1, Pallas kernels: 51.1 us -> 48 us  [body(): pl.pallas_call(main_kernel, out_shape=(jax.ShapeDtypeStruct((1, width), f...]
    unnamed x6 -> x0, local copies, waits for them, and re-layouts: 2.87 us -> none
where the time goes in v2:
time: 55.3 us; the launch traced here: 55.1 us
  Pallas kernels  52.1 us (94%)
  between operations  3.04 us (5%)
    pallas_call x1, Pallas kernels, body(): pl.pallas_call(main_kernel, out_shape=(jax.ShapeDtypeStruct((1, width), f...  48 us
    pallas_call x1, Pallas kernels, body(): pl.pallas_call(out_kernel, grid=(length_rows // ROWS,), out_shape=jax.Sha...  4.08 us

profile of v2, /device:TPU:1, one launch (start us, length us, event | category | flops | bytes accessed | tf_op | source)
XLA Modules:
  0.0 55.1 jit_solution(7656007836219466634)
XLA Ops:
  1.3 48.0 %main.1 = (f32[1,3584]{1,0:T(1,128)}, f32[256,128]{1,0:T(8,128)}, f32[1,1]{1,0:T(1,128)}) custom-call(bf16[1,256,3584]{2,1,0:T(8,128)(2,1)} %hidden.3, s32[1]{0:T(128)S(6)} %copy.8.lengths_h, s32[384]{0:T(512)} %perm_h.1, bf16[3584]{0:T(1024)(128)(2,1)} %gain_h.1, bf16[3584,1024]{1,0:T(8,128)(2,1)} %proj_h.1), custom_call_target="tpu_custom_call" | custom-call | tf_op jit(solution)/shard_map/main/pallas_call | solution.py:302
  49.3 4.1 %hidden_grad.1 = bf16[1,256,3584]{2,1,0:T(8,128)(2,1)} custom-call(bf16[1,256,3584]{2,1,0:T(8,128)(2,1)} %hidden.3, f32[1,3584]{1,0:T(1,128)} %get-tuple-element.5.g, f32[256,128]{1,0:T(8,128)} %get-tuple-element.6.coef), custom_call_target="tpu_custom_call" | custom-call | tf_op jit(solution)/shard_map/hidden_grad/pallas_call | solution.py:335

commit v3 on v2

--- a/solution.py
+++ b/solution.py
@@ -19,6 +19,7 @@
 
 NX, NY, NZ = 4, 8, 12
 ROWS = 64
+OUT_ROWS = 32
 PROJ = 512
 
 XC = [(x, 0, 0, c) for x in range(NX) for c in range(2) if (x, c) != (0, 0)]
@@ -191,23 +192,24 @@
 
     pl.when(z_hi == 0)(prepare)
 
-    sent = []
-
     def copy(k, ref, d):
         out = pltpu.make_async_remote_copy(
             src_ref=ref, dst_ref=ref, send_sem=send_sem.at[k], recv_sem=recv_sem.at[k],
             device_id=device(d), device_id_type=MESH,
         )
         out.start()
-        sent.append(out)
         return out
+
+    def sent(copies):
+        for c in copies:
+            c.wait_send()
 
     def tile(q):
         return pl.ds(pl.multiple_of(core * 512 + (q % 4) * 128, 128), 128)
 
     pl.semaphore_wait(barrier, len(PEERS))
-    arriving = [copy(i, packets.at[my_rows], d) for i, d in enumerate(XC)]
-    for c in arriving:
+    rows_in = [copy(i, packets.at[my_rows], d) for i, d in enumerate(XC)]
+    for c in rows_in:
         c.wait_recv()
     block = emb.at[z_hi, y_far, y_par, z_lo]
     for k in range(8):
@@ -217,8 +219,9 @@
             block[:, k * 128 : (k + 1) * 128] = part.astype(bf16)
 
     cut = emb.at[z_hi, y_far, y_par, z_lo, :, tile(x)]
-    arriving = [copy(AT_FAR + i, cut, d) for i, d in enumerate(FAR)]
-    for c in arriving:
+    far_in = [copy(AT_FAR + i, cut, d) for i, d in enumerate(FAR)]
+    sent(rows_in)
+    for c in far_in:
         c.wait_recv()
 
     near = []
@@ -241,12 +244,18 @@
             copy(base + j, emb.at[:, pl.ds(*part), par, lo, :, cols], d)
             for j, (d, part) in enumerate(LAST)
         ])
+        if i == 0:
+            sent(far_in)
+    for copies in near:
+        sent(copies)
     half = pl.ds(pl.multiple_of(core * 512, 512), 512)
     arriving = []
     for i, (par, lo) in enumerate(classes):
         for c in neighbours[i]:
             c.wait_recv()
         arriving.append(copy(AT_SIB + 4 * par + lo, emb.at[:, :, par, lo, :, half], SIBLING))
+    for copies in neighbours:
+        sent(copies)
     pl.when(z_hi != 0)(prepare)
     for c in arriving:
         c.wait_recv()
@@ -287,12 +296,29 @@
     dots = jnp.sum(xg_proj[...] * grad_rows[0:1].astype(f32), axis=1, keepdims=True)
     lane = lax.broadcasted_iota(jnp.int32, coef_out.shape, 1)
     coef_out[...] = jnp.where(lane == 1, coef_out[...] * dots, coef_out[...])
-    for c in sent:
+    for c in arriving:
         c.wait_send()
 
 
-def out_kernel(hidden, g, coef, out):
-    out[0] = (coef[:, 0:1] * g[...] - hidden[0].astype(f32) * coef[:, 1:2]).astype(bf16)
+def out_kernel(hidden, g_h, coef_h, out, x_v, g, coef, o_v, in_sem, out_sem):
+    n, rows = x_v.shape[0] // OUT_ROWS, [pl.ds(i, OUT_ROWS) for i in range(0, x_v.shape[0], OUT_ROWS)]
+    small = [
+        pltpu.make_async_copy(g_h, g, in_sem.at[n]),
+        pltpu.make_async_copy(coef_h, coef, in_sem.at[n + 1]),
+    ]
+    loads = [pltpu.make_async_copy(hidden.at[0, r], x_v.at[r], in_sem.at[i]) for i, r in enumerate(rows)]
+    stores = [pltpu.make_async_copy(o_v.at[r], out.at[0, r], out_sem.at[i]) for i, r in enumerate(rows)]
+    for c in small + loads:
+        c.start()
+    for c in small:
+        c.wait()
+    for r, load, store in zip(rows, loads, stores):
+        load.wait()
+        grad = coef[r, 0:1] * g[...] - x_v[r, :].astype(f32) * coef[r, 1:2]
+        o_v[r, :] = grad.astype(bf16)
+        store.start()
+    for store in stores:
+        store.wait()
 
 
 def body(hidden, lengths, pair_perm, norm_gain, projection):
@@ -332,16 +358,20 @@
         ),
         name="main",
     )(hidden, lengths, pair_perm, norm_gain, projection)
+    n_out = length_rows // OUT_ROWS
     grad = pl.pallas_call(
         out_kernel,
-        grid=(length_rows // ROWS,),
         out_shape=jax.ShapeDtypeStruct(hidden.shape, bf16),
-        in_specs=[
-            pl.BlockSpec((1, ROWS, width), lambda i: (0, i, 0)),
-            pl.BlockSpec((1, width), lambda i: (0, 0)),
-            pl.BlockSpec((ROWS, 128), lambda i: (i, 0)),
+        in_specs=[HBM] * 3,
+        out_specs=HBM,
+        scratch_shapes=[
+            pltpu.VMEM((length_rows, width), bf16),
+            pltpu.VMEM((1, width), f32),
+            pltpu.VMEM((length_rows, 128), f32),
+            pltpu.VMEM((length_rows, width), bf16),
+            pltpu.SemaphoreType.DMA((n_out + 2,)),
+            pltpu.SemaphoreType.DMA((n_out,)),
         ],
-        out_specs=pl.BlockSpec((1, ROWS, width), lambda i: (0, i, 0)),
         compiler_params=pltpu.CompilerParams(vmem_limit_bytes=60 << 20),
         name="hidden_grad",
     )(hidden, g, coef)

time: 55.3 us -> 54.2 us (0.980)
  Pallas kernels: 52.1 us -> 50.9 us
    pallas_call x1, Pallas kernels: 4.08 us -> 3.05 us  [body(): pl.pallas_call(out_kernel, out_shape=jax.ShapeDtypeStruct(hidden.shape, b...]
where the time goes in v3:
time: 54.2 us; the launch traced here: 54 us
  Pallas kernels  50.9 us (94%)
  between operations  3.04 us (6%)
    pallas_call x1, Pallas kernels, body(): pl.pallas_call(main_kernel, out_shape=(jax.ShapeDtypeStruct((1, width), f...  47.9 us
    pallas_call x1, Pallas kernels, body(): pl.pallas_call(out_kernel, out_shape=jax.ShapeDtypeStruct(hidden.shape, b...  3.05 us

profile of v3, /device:TPU:1, one launch (start us, length us, event | category | flops | bytes accessed | tf_op | source)
XLA Modules:
  0.0 54.0 jit_solution(9897043308371274952)
XLA Ops:
  1.3 47.9 %main.1 = (f32[1,3584]{1,0:T(1,128)}, f32[256,128]{1,0:T(8,128)}, f32[1,1]{1,0:T(1,128)}) custom-call(bf16[1,256,3584]{2,1,0:T(8,128)(2,1)} %hidden.3, s32[1]{0:T(128)S(6)} %copy.8.lengths_h, s32[384]{0:T(512)} %perm_h.1, bf16[3584]{0:T(1024)(128)(2,1)} %gain_h.1, bf16[3584,1024]{1,0:T(8,128)(2,1)} %proj_h.1), custom_call_target="tpu_custom_call" | custom-call | tf_op jit(solution)/shard_map/main/pallas_call | solution.py:328
  49.1 3.1 %hidden_grad.1 = bf16[1,256,3584]{2,1,0:T(8,128)(2,1)} custom-call(bf16[1,256,3584]{2,1,0:T(8,128)(2,1)} %hidden.3, f32[1,3584]{1,0:T(1,128)} %get-tuple-element.5.g_h, f32[256,128]{1,0:T(8,128)} %get-tuple-element.6.coef_h), custom_call_target="tpu_custom_call" | custom-call | tf_op jit(solution)/shard_map/hidden_grad/pallas_call | solution.py:362

commit v4 on v3

--- a/solution.py
+++ b/solution.py
@@ -70,7 +70,7 @@
 def main_kernel(
     hidden, lengths_h, perm_h, gain_h, proj_h,
     g_out, coef_out, loss_out,
-    lengths, perm_s, perm_v, x_v, proj, proj_t, gain_v, gain_f, packets, emb, target, pooled_v, xg_proj,
+    lengths, perm_s, perm_v, x_v, proj, proj_t, gain_v, gain_f, pieces, rows8, emb, target, score_v, pooled_v, xg_proj,
     in_sem, small_sem, send_sem, recv_sem,
 ):
     z_hi = lax.axis_index("section")
@@ -152,13 +152,10 @@
     magnitude = jnp.sqrt(jnp.sum(raw * raw, axis=1, keepdims=True) + EPS)
     unit = raw / magnitude
     own = unit.astype(bf16)
-    sub = lax.broadcasted_iota(jnp.int32, (8, 128), 0)
-    packet = jnp.zeros((8, 128), f32)
+    mine = x * 2 + core
+    kept = core * 4 + x
     for k in range(8):
-        packet = jnp.where(sub == k, own[:, k * 128 : (k + 1) * 128].astype(f32), packet)
-    mine = x * 2 + core
-    my_rows = pl.ds(pl.multiple_of(mine * 8, 8), 8)
-    packets[my_rows, :] = packet
+        pieces[k] = own[0:1, k * 128 : (k + 1) * 128].astype(f32)
 
     for c in small[2:]:
         c.wait()
@@ -192,9 +189,9 @@
 
     pl.when(z_hi == 0)(prepare)
 
-    def copy(k, ref, d):
+    def copy(k, ref, d, src=None):
         out = pltpu.make_async_remote_copy(
-            src_ref=ref, dst_ref=ref, send_sem=send_sem.at[k], recv_sem=recv_sem.at[k],
+            src_ref=ref if src is None else src, dst_ref=ref, send_sem=send_sem.at[k], recv_sem=recv_sem.at[k],
             device_id=device(d), device_id_type=MESH,
         )
         out.start()
@@ -208,15 +205,15 @@
         return pl.ds(pl.multiple_of(core * 512 + (q % 4) * 128, 128), 128)
 
     pl.semaphore_wait(barrier, len(PEERS))
-    rows_in = [copy(i, packets.at[my_rows], d) for i, d in enumerate(XC)]
+    rows_in = [
+        copy(i, rows8.at[mine], d, pieces.at[(core + d[3]) % 2 * 4 + (x + d[0]) % NX])
+        for i, d in enumerate(XC)
+    ]
+    rows8[mine] = pieces[kept]
     for c in rows_in:
         c.wait_recv()
     block = emb.at[z_hi, y_far, y_par, z_lo]
-    for k in range(8):
-        @pl.when(k == core * 4 + x)
-        def _(k=k):
-            part = packets[pl.ds(k, 8, stride=8), :]
-            block[:, k * 128 : (k + 1) * 128] = part.astype(bf16)
+    block[:, tile(x)] = rows8[...].reshape(8, 128).astype(bf16)
 
     cut = emb.at[z_hi, y_far, y_par, z_lo, :, tile(x)]
     far_in = [copy(AT_FAR + i, cut, d) for i, d in enumerate(FAR)]
@@ -266,8 +263,7 @@
     exps = jnp.exp(scores)
     code_totals = jnp.sum(exps, axis=1, keepdims=True)
     doc_totals = jnp.sum(exps, axis=0, keepdims=True)
-    log_sum = jnp.sum(jnp.log(doc_totals)) + jnp.sum(jnp.log(code_totals))
-    loss_out[0, 0] = (log_sum - 2.0 * jnp.sum(target[...] * scores)) / (2 * pairs)
+    score_v[...] = scores
     code_row = jnp.broadcast_to(code_totals, (pairs, 128)).T[0:1, :]
 
     me = z_hi * (pairs * 2 // 3) + dp
@@ -296,6 +292,8 @@
     dots = jnp.sum(xg_proj[...] * grad_rows[0:1].astype(f32), axis=1, keepdims=True)
     lane = lax.broadcasted_iota(jnp.int32, coef_out.shape, 1)
     coef_out[...] = jnp.where(lane == 1, coef_out[...] * dots, coef_out[...])
+    log_sum = jnp.sum(jnp.log(doc_totals) + jnp.log(code_row))
+    loss_out[0, 0] = (log_sum - 2.0 * jnp.sum(target[...] * score_v[...])) / (2 * pairs)
     for c in arriving:
         c.wait_send()
 
@@ -343,8 +341,10 @@
             pltpu.VMEM((embed, width), bf16),
             pltpu.VMEM((width,), bf16),
             pltpu.VMEM((1, width), f32),
-            pltpu.VMEM((64, 128), f32),
+            pltpu.VMEM((8, 1, 128), f32),
+            pltpu.VMEM((8, 1, 128), f32),
             pltpu.VMEM((3, 4, 2, 4, 8, embed), bf16),
+            pltpu.VMEM((pairs, pairs), f32),
             pltpu.VMEM((pairs, pairs), f32),
             pltpu.VMEM((16, width), bf16),
             pltpu.VMEM((length_rows, embed), f32),

time: 54.2 us -> 54.1 us (level)
  no operation moved by 1% of the time
where the time goes in v4:
time: 54.1 us; the launch traced here: 53.9 us
  Pallas kernels  50.8 us (94%)
  between operations  3.04 us (6%)
    pallas_call x1, Pallas kernels, body(): pl.pallas_call(main_kernel, out_shape=(jax.ShapeDtypeStruct((1, width), f...  47.8 us
    pallas_call x1, Pallas kernels, body(): pl.pallas_call(out_kernel, out_shape=jax.ShapeDtypeStruct(hidden.shape, b...  3.05 us

profile of v4, /device:TPU:1, one launch (start us, length us, event | category | flops | bytes accessed | tf_op | source)
XLA Modules:
  0.0 53.9 jit_solution(7465022579781684657)
XLA Ops:
  1.3 47.8 %main.1 = (f32[1,3584]{1,0:T(1,128)}, f32[256,128]{1,0:T(8,128)}, f32[1,1]{1,0:T(1,128)}) custom-call(bf16[1,256,3584]{2,1,0:T(8,128)(2,1)} %hidden.3, s32[1]{0:T(128)S(6)} %copy.8.lengths_h, s32[384]{0:T(512)} %perm_h.1, bf16[3584]{0:T(1024)(128)(2,1)} %gain_h.1, bf16[3584,1024]{1,0:T(8,128)(2,1)} %proj_h.1), custom_call_target="tpu_custom_call" | custom-call | tf_op jit(solution)/shard_map/main/pallas_call | solution.py:326
  49.0 3.1 %hidden_grad.1 = bf16[1,256,3584]{2,1,0:T(8,128)(2,1)} custom-call(bf16[1,256,3584]{2,1,0:T(8,128)(2,1)} %hidden.3, f32[1,3584]{1,0:T(1,128)} %get-tuple-element.5.g_h, f32[256,128]{1,0:T(8,128)} %get-tuple-element.6.coef_h), custom_call_target="tpu_custom_call" | custom-call | tf_op jit(solution)/shard_map/hidden_grad/pallas_call | solution.py:362
